TPU v7x, 512 devices: a whole 4x8x8 slice. The times are simulated.
512 devices in a mesh: tm: 32 (over y_lo, z), tensor: 16 (over x, y_hi, core).
Axes of the slice: x: 4, y: 8 (y_hi: 2, y_lo: 4; y = y_hi * 4 + y_lo), z: 8, core: 2. Of those that a mesh axis runs over, the one named last changes fastest.
Arguments:
- tokens: bfloat16 [64, 256, 4096], P('tm'), may hold values from -200 to 200
- norm_gain: float32 [4096], replicated, may hold values from 0.1 to 1.9
- q_gain: float32 [32, 128], P('tensor'), may hold values from 0.5 to 2
- k_gain: float32 [32, 128], P('tensor'), may hold values from 0.5 to 2
- w_qkv: bfloat16 [3, 4096, 4096], P(None, 'tm', 'tensor'), may hold values from -0.09375 to 0.09375
- w_out: bfloat16 [4096, 4096], P('tensor', 'tm'), may hold values from -0.1875 to 0.1875
Outputs:
- mixed: bfloat16 [64, 256, 4096], P('tm', None, 'tensor')
All inputs are finite; a program needn't handle non-finite values.
Results may differ from a plain program's by a relative error of at most 0.018.
Values may be sent and summed in bfloat16 or wider, within the bound.
A program may use at most 64 MiB of HBM per device.

v0:
```python
import jax
import jax.numpy as jnp
from jax import lax
from jax.sharding import PartitionSpec as P

FRAMES = 16


def head_norm(raw, gain):
    scale = lax.rsqrt(jnp.mean(raw * raw, axis=-1, keepdims=True) + 1e-06)
    return raw * scale * gain


def attend(block):
    rows_all = block.shape[1]
    clips = rows_all // FRAMES
    shape = (clips, FRAMES) + block.shape[2:]
    query = block[0].reshape(shape)
    key = block[1].reshape(shape)
    value = block[2].reshape(shape)
    head_size = block.shape[-1]
    scores = jnp.einsum(
        "cfphd,cgphd->cphfg", query, key, preferred_element_type=jnp.float32
    ) / jnp.sqrt(jnp.float32(head_size))
    frame_ids = jnp.arange(FRAMES, dtype=jnp.int32)
    causal = frame_ids[:, None] >= frame_ids[None, :]
    expo = jnp.where(causal, jnp.exp(scores), jnp.float32(0.0))
    weights = (expo / jnp.sum(expo, axis=-1, keepdims=True)).astype(jnp.bfloat16)
    attended = jnp.einsum("cphfg,cgphd->cfphd", weights, value, preferred_element_type=jnp.float32)
    return attended.astype(jnp.bfloat16).reshape(block.shape[1:])


def body(tokens, norm_gain, q_gain, k_gain, w_qkv, w_out):
    frames_dev, patches, width = tokens.shape
    heads_dev, head_size = q_gain.shape
    local = heads_dev * head_size
    values = tokens.astype(jnp.float32)
    meansq = jnp.mean(values * values, axis=-1, keepdims=True)
    normed = (values * lax.rsqrt(meansq + 1e-06) * norm_gain).astype(jnp.bfloat16)
    spread = lax.all_to_all(normed, "tm", split_axis=1, concat_axis=0, tiled=True)
    rows_all, patch_dev = (spread.shape[0], spread.shape[1])
    rows_in = spread.reshape(rows_all * patch_dev, width)
    count = rows_in.shape[0]
    raw = jnp.einsum(
        "tr,xrc->xtc",
        rows_in,
        lax.all_gather(w_qkv, "tm", axis=1, tiled=True),
        preferred_element_type=jnp.float32,
    )
    raw = raw.reshape(3, count, heads_dev, head_size)
    query = head_norm(raw[0], q_gain)
    key = head_norm(raw[1], k_gain)
    stacked = jnp.stack([query, key, raw[2]]).astype(jnp.bfloat16)
    stacked = stacked.reshape(3, rows_all, patch_dev, heads_dev, head_size)
    mixed_heads = attend(stacked)
    attended = lax.all_to_all(mixed_heads, "tm", split_axis=0, concat_axis=1, tiled=True)
    attended = attended.reshape(frames_dev * patches, local)
    terms = jnp.dot(
        attended,
        lax.all_gather(w_out, "tm", axis=1, tiled=True),
        preferred_element_type=jnp.float32,
    )
    mixed = lax.psum_scatter(terms.astype(jnp.bfloat16), "tensor", scatter_dimension=1, tiled=True)
    return mixed.reshape(frames_dev, patches, -1)


def solution(mesh):
    placed = (
        P("tm", None, None),
        P(),
        P("tensor", None),
        P("tensor", None),
        P(None, "tm", "tensor"),
        P("tensor", "tm"),
    )
    return jax.shard_map(
        body, mesh=mesh, in_specs=placed, out_specs=P("tm", None, "tensor"), check_vma=False
    )
```

profile of v0, /device:TPU:1, one launch (start us, length us, event | category | flops | bytes accessed | tf_op | source)
XLA Modules:
  0.0 523.8 jit_solution(4048171896761189357)
XLA Ops:
  6.5 0.0 copy-start.1
  6.5 0.0 all-gather.3.cloned.1.call-start
  6.5 1.8 copy.36
  8.3 0.0 all-gather.3.cloned.1.call-update
  8.3 0.0 copy-start
  8.3 3.2 fusion
  11.6 0.0 copy-done.1
  11.6 0.2 copy-done
  11.8 1.6 fusion.2
  13.4 6.5 %copy.34 = bf16[2,256,4096]{2,0,1:T(2,128)(2,1)} copy(bf16[2,256,4096]{2,1,0:T(8,128)(2,1)S(1)} %fusion.2) | data formatting | bytes 8388608 | tf_op jit(solution)/shard_map/convert_element_type | solution.py:39
  19.9 14.4 %all-to-all-start = ((bf16[2,256,4096]{2,0,1:T(2,128)(2,1)}), bf16[2,256,4096]{2,0,1:T(2,128)(2,1)}, u32[]{:S(2)}, u32[]{:S(2)}) async-start(bf16[2,256,4096]{2,0,1:T(2,128)(2,1)} %copy.34), calls=%async_computation | async-start | bytes 8388608 | tf_op jit(solution)/shard_map/all_to_all | solution.py:40
  34.3 0.0 all-gather.5.cloned.1.call-start
  34.4 0.7 all-gather.5.cloned.1.call-update
  35.1 0.2 reduce-scatter.2.cloned.1.call-start
  35.3 114.9 %all-to-all-done = bf16[2,256,4096]{2,0,1:T(2,128)(2,1)} async-done(((bf16[2,256,4096]{2,0,1:T(2,128)(2,1)}), bf16[2,256,4096]{2,0,1:T(2,128)(2,1)}, u32[]{:S(2)}, u32[]{:S(2)}) %all-to-all-start) | async-done | bytes 4194336 | tf_op jit(solution)/shard_map/all_to_all | solution.py:40
  150.2 8.7 %copy.35 = bf16[2,32,8,4096]{3,2,0,1:T(8,128)(2,1)} copy(bf16[2,32,8,4096]{3,0,2,1:T(2,128)(2,1)} %bitcast) | data formatting | bytes 8388608 | tf_op jit(solution)/shard_map/all_to_all | solution.py:40
  158.9 98.1 %all-gather.3.cloned.1.call-done = bf16[3,4096,256]{1,2,0:T(8,128)(2,1)} async-done(((bf16[3,128,256]{1,2,0:T(8,128)(2,1)}), bf16[3,4096,256]{1,2,0:T(8,128)(2,1)}) %all-gather.3.cloned.1.call-update) | async-done | bytes 6291472 | tf_op jit(solution)/shard_map/all_gather | solution.py:47
  257.0 6.8 %convolution_bitcast_fusion = f32[3,512,256]{1,2,0:T(8,128)S(1)} fusion(bf16[512,4096,1]{1,0,2:T(8,128)(2,1)} %bitcast.28, bf16[3,4096,256]{1,2,0:T(8,128)(2,1)} %all-gather.3.cloned.1.call-done), kind=kOutput, calls=%fused_computation.6 | convolution fusion | flops 3221225472 | bytes 12058624 | tf_op jit(solution)/shard_map/tr,xrc->xtc/dot_general | solution.py:44
  263.9 0.0 copy-start.2
  263.9 0.0 copy-start.3
  263.9 0.3 slice_multiply_fusion.1
  264.2 0.2 copy.38
  264.4 0.2 copy.39
  264.6 0.1 reduce_sum.37
  264.7 0.1 copy.37
  264.9 0.0 copy-done.2
  264.9 0.2 multiply_convert_fusion.1
  265.1 0.0 copy-done.3
  265.1 0.2 multiply_convert_fusion
  265.3 0.3 fusion.4
  265.6 0.3 fusion.5
  265.9 0.1 copy.44
  266.0 16.4 %all_to_all.30 = bf16[64,8,2,128]{3,1,2,0:T(8,128)(2,1)S(1)} all-to-all(bf16[64,8,2,128]{3,1,2,0:T(8,128)(2,1)S(1)} %bitcast.34), channel_id=1, replica_groups=mesh['tm'=32,'tensor'=16] {'tm'}, dimensions={0} | all-to-all | bytes 524288 | tf_op jit(solution)/shard_map/all_to_all | solution.py:56
  282.5 106.2 %all-gather.5.cloned.1.call-done = bf16[256,4096]{1,0:T(8,128)(2,1)} async-done(((bf16[256,128]{1,0:T(8,128)(2,1)}), bf16[256,4096]{1,0:T(8,128)(2,1)}) %all-gather.5.cloned.1.call-update) | async-done | bytes 2097168 | tf_op jit(solution)/shard_map/all_gather | solution.py:60
  388.6 4.8 convolution_convert_fusion
  393.4 0.0 reduce-scatter.2.cloned.1.call-update
  393.4 123.9 %reduce-scatter.2.cloned.1.call-done = bf16[512,256]{1,0:T(8,128)(2,1)} async-done(((bf16[512,4096]{1,0:T(8,128)(2,1)}), bf16[512,256]{1,0:T(8,128)(2,1)}) %reduce-scatter.2.cloned.1.call-update) | async-done | bytes 262160 | tf_op jit(solution)/shard_map/reduce_scatter | solution.py:63
  (7 shorter events, 0.1 us)
Async XLA Ops:
  6.5 5.0 copy-start.1
  6.5 250.5 %all-gather.3.cloned.1.call-start = ((), (), s32[]{:S(2)}) async-start(), calls=%async_computation.3 | async-start | bytes 6488064 | tf_op jit(solution)/shard_map/all_gather | solution.py:47
  8.3 3.5 copy-start
  19.9 130.3 %all-to-all-start = ((bf16[2,256,4096]{2,0,1:T(2,128)(2,1)}), bf16[2,256,4096]{2,0,1:T(2,128)(2,1)}, u32[]{:S(2)}, u32[]{:S(2)}) async-start(bf16[2,256,4096]{2,0,1:T(2,128)(2,1)} %copy.34), calls=%async_computation | async-start | bytes 8388608 | tf_op jit(solution)/shard_map/all_to_all | solution.py:40
  34.3 354.3 %all-gather.5.cloned.1.call-start = ((), (), s32[]{:S(2)}) async-start(), calls=%async_computation.4 | async-start | bytes 2162688 | tf_op jit(solution)/shard_map/all_gather | solution.py:60
  35.1 482.2 %reduce-scatter.2.cloned.1.call-start = ((), (), s32[]{:S(2)}) async-start(), calls=%async_computation.5 | async-start | bytes 4456448 | tf_op jit(solution)/shard_map/reduce_scatter | solution.py:63
  263.9 1.0 copy-start.2
  263.9 1.2 copy-start.3
Sparse Core Ops, SparseCore 0:
  9.4 247.6 all-gather.2
  259.0 129.5 all-gather.4
  393.6 123.6 reduce-scatter.1
where the time goes:
time: 524 us
  waiting for transfers between devices  444 us (85%)
  local copies, waits for them, and re-layouts  17.9 us (3%)
  blocking collectives  16.4 us (3%)
  starting transfers between devices  14.7 us (3%)
  between operations  13.3 us (3%)
  matrix products  12.2 us (2%)
  other arithmetic  5.66 us (1%)
    reduce_scatter x1, waiting for transfers between devices, body(): lax.psum_scatter(terms.astype(jnp.bfloat16), 'tensor', scatter_dimension=...  124 us
    all_to_all x1, waiting for transfers between devices, body(): lax.all_to_all(normed, 'tm', split_axis=1, concat_axis=0, tiled=True)  115 us
    all_gather x1, waiting for transfers between devices, body(): lax.all_gather(w_out, 'tm', axis=1, tiled=True)  106 us
    all_gather x1, waiting for transfers between devices, body(): lax.all_gather(w_qkv, 'tm', axis=1, tiled=True)  98.1 us
    all_to_all x1, blocking collectives, body(): lax.all_to_all(mixed_heads, 'tm', split_axis=0, concat_axis=1, tiled=True)  16.4 us
    all_to_all x1, starting transfers between devices, body(): lax.all_to_all(normed, 'tm', split_axis=1, concat_axis=0, tiled=True)  14.4 us
  transfers between devices with their start and end apart: 4, of which 4 were waited for; matrix products, arithmetic and copies ran while one was open for 6% of the time, Pallas kernels for 0%

commit v1 on v0

v1 whole, which is shorter than its diff:
```python
import jax
import jax.numpy as jnp
from jax import lax
from jax.sharding import PartitionSpec as P

FRAMES = 16


def head_norm(raw, gain):
    scale = lax.rsqrt(jnp.mean(raw * raw, axis=-1, keepdims=True) + 1e-06)
    return raw * scale * gain


def attend(query, key, value):
    head_size = query.shape[-1]
    scores = jnp.einsum(
        "fphd,gphd->phfg", query, key, preferred_element_type=jnp.float32
    ) / jnp.sqrt(jnp.float32(head_size))
    frame_ids = jnp.arange(FRAMES, dtype=jnp.int32)
    causal = frame_ids[:, None] >= frame_ids[None, :]
    expo = jnp.where(causal, jnp.exp(scores), jnp.float32(0.0))
    weights = (expo / jnp.sum(expo, axis=-1, keepdims=True)).astype(jnp.bfloat16)
    attended = jnp.einsum("phfg,gphd->fphd", weights, value, preferred_element_type=jnp.float32)
    return attended.astype(jnp.bfloat16)


def body(tokens, norm_gain, q_gain, k_gain, w_qkv, w_out):
    frames_dev, patches, width = tokens.shape
    heads_dev, head_size = q_gain.shape
    local = heads_dev * head_size
    count = frames_dev * patches
    share = FRAMES // frames_dev
    clips = lax.axis_size("tm") // share
    groups = [[c * share + i for i in range(share)] for c in range(clips)]
    values = tokens.astype(jnp.float32)
    meansq = jnp.mean(values * values, axis=-1, keepdims=True)
    normed = (values * lax.rsqrt(meansq + 1e-06) * norm_gain).astype(jnp.bfloat16)
    raw = jnp.einsum(
        "tr,xrc->xtc",
        normed.reshape(count, width),
        lax.all_gather(w_qkv, "tm", axis=1, tiled=True),
        preferred_element_type=jnp.float32,
    )
    raw = raw.reshape(3, count, heads_dev, head_size)
    query = head_norm(raw[0], q_gain)
    key = head_norm(raw[1], k_gain)
    stacked = jnp.stack([query, key, raw[2]]).astype(jnp.bfloat16)
    stacked = stacked.reshape(3, frames_dev, patches, heads_dev, head_size)
    stacked = lax.all_to_all(
        stacked, "tm", split_axis=2, concat_axis=1, tiled=True, axis_index_groups=groups
    )
    mixed_heads = attend(stacked[0], stacked[1], stacked[2])
    attended = lax.all_to_all(
        mixed_heads, "tm", split_axis=0, concat_axis=1, tiled=True, axis_index_groups=groups
    )
    terms = jnp.dot(
        attended.reshape(count, local),
        lax.all_gather(w_out, "tm", axis=1, tiled=True),
        preferred_element_type=jnp.float32,
    )
    mixed = lax.psum_scatter(terms.astype(jnp.bfloat16), "tensor", scatter_dimension=1, tiled=True)
    return mixed.reshape(frames_dev, patches, -1)


def solution(mesh):
    placed = (
        P("tm", None, None),
        P(),
        P("tensor", None),
        P("tensor", None),
        P(None, "tm", "tensor"),
        P("tensor", "tm"),
    )
    return jax.shard_map(
        body, mesh=mesh, in_specs=placed, out_specs=P("tm", None, "tensor"), check_vma=False
    )
```

time: 524 us -> 421 us (0.80)
  waiting for transfers between devices: 444 us -> 355 us
  local copies, waits for them, and re-layouts: 17.9 us -> 8.47 us
  starting transfers between devices: 14.7 us -> 5.81 us
    all_to_all x1, waiting for transfers between devices: 115 us -> 14.9 us  [body(): lax.all_to_all(stacked, 'tm', split_axis=2, concat_axis=1, tiled=True, ax...]
    all_gather x1, waiting for transfers between devices: 98.1 us -> 135 us  [body(): lax.all_gather(w_qkv, 'tm', axis=1, tiled=True)]
    all_gather x1, waiting for transfers between devices: 106 us -> 80.1 us  [body(): lax.all_gather(w_out, 'tm', axis=1, tiled=True)]
    all_to_all x1, starting transfers between devices: 14.4 us -> 5.73 us  [body(): lax.all_to_all(stacked, 'tm', split_axis=2, concat_axis=1, tiled=True, ax...]
    all_to_all x2, local copies, waits for them, and re-layouts: 8.76 us -> 0.32 us  [the longest x1 0.2 us: body(): lax.all_to_all(mixed_heads, 'tm', split_axis=0, concat_axis=1, tiled=True...]
    convert_element_type x2 -> x1, local copies, waits for them, and re-layouts: 6.58 us -> 0.25 us  [attend(): return attended.astype(jnp.bfloat16)]
where the time goes in v1:
time: 421 us
  waiting for transfers between devices  355 us (84%)
  blocking collectives  15.6 us (4%)
  between operations  13.3 us (3%)
  matrix products  12.2 us (3%)
  other arithmetic  10.7 us (3%)
  local copies, waits for them, and re-layouts  8.47 us (2%)
  starting transfers between devices  5.81 us (1%)
    all_gather x1, waiting for transfers between devices, body(): lax.all_gather(w_qkv, 'tm', axis=1, tiled=True)  135 us
    reduce_scatter x1, waiting for transfers between devices, body(): lax.psum_scatter(terms.astype(jnp.bfloat16), 'tensor', scatter_dimension=...  124 us
    all_gather x1, waiting for transfers between devices, body(): lax.all_gather(w_out, 'tm', axis=1, tiled=True)  80.1 us
    all_to_all x1, blocking collectives, body(): lax.all_to_all(mixed_heads, 'tm', split_axis=0, concat_axis=1, tiled=True...  15.6 us
    all_to_all x1, waiting for transfers between devices, body(): lax.all_to_all(stacked, 'tm', split_axis=2, concat_axis=1, tiled=True, ax...  14.9 us
  transfers between devices with their start and end apart: 4, of which 4 were waited for; matrix products, arithmetic and copies ran while one was open for 6% of the time, Pallas kernels for 0%

profile of v1, /device:TPU:1, one launch (start us, length us, event | category | flops | bytes accessed | tf_op | source)
XLA Modules:
  0.0 420.7 jit_solution(8180286489169808993)
XLA Ops:
  6.5 0.0 all-gather.3.cloned.1.call-start
  6.5 1.8 copy.28
  8.3 0.0 all-gather.3.cloned.1.call-update
  8.3 0.0 all-gather.5.cloned.1.call-start
  8.4 0.7 all-gather.5.cloned.1.call-update
  9.1 0.0 copy-start
  9.1 3.2 fusion
  12.3 0.0 copy-done.2
  12.3 0.2 copy-done
  12.5 3.6 fusion.2
  16.2 135.3 %all-gather.3.cloned.1.call-done = bf16[3,4096,256]{1,2,0:T(8,128)(2,1)} async-done(((bf16[3,128,256]{1,2,0:T(8,128)(2,1)}), bf16[3,4096,256]{1,2,0:T(8,128)(2,1)}) %all-gather.3.cloned.1.call-update) | async-done | bytes 6291472 | tf_op jit(solution)/shard_map/all_gather | solution.py:41
  151.4 6.8 %convolution_bitcast_fusion = f32[3,512,256]{1,2,0:T(8,128)S(1)} fusion(bf16[512,4096,1]{1,0,2:T(8,128)(2,1)} %bitcast.38, bf16[3,4096,256]{1,2,0:T(8,128)(2,1)} %all-gather.3.cloned.1.call-done), kind=kOutput, calls=%fused_computation.6 | convolution fusion | flops 3221225472 | bytes 12058624 | tf_op jit(solution)/shard_map/tr,xrc->xtc/dot_general | solution.py:38
  158.3 1.2 copy-done.1
  159.4 0.2 slice_multiply_fusion.1
  159.7 0.0 copy-start.3
  159.7 0.0 copy-start.4
  159.7 0.1 reduce_sum.37
  159.8 1.1 slice.40
  160.9 0.3 squeeze.15
  161.2 0.6 copy.30
  161.8 0.3 squeeze.16
  162.2 0.6 copy.32
  162.8 0.2 copy.29
  163.0 0.1 reduce_sum.38
  163.1 0.2 copy.31
  163.3 0.1 stack.7
  163.3 0.5 copy.33
  163.8 0.0 copy-done.3
  163.8 0.0 copy-done.4
  163.9 1.4 multiply_convert_fusion
  165.3 2.0 pad_maximum_fusion
  167.3 5.7 %all-to-all-start = ((bf16[3,2,256,2,128]{4,3,1,0,2:T(2,128)(2,1)}), bf16[3,2,256,2,128]{4,3,1,0,2:T(2,128)(2,1)S(1)}, u32[]{:S(2)}, u32[]{:S(2)}) async-start(bf16[3,2,256,2,128]{4,3,1,0,2:T(2,128)(2,1)} %pad_maximum_fusion), calls=%async_computation | async-start | bytes 1572864 | tf_op jit(solution)/shard_map/all_to_all | solution.py:49
  173.0 0.0 reduce-scatter.2.cloned.1.call-start
  173.1 14.9 %all-to-all-done = bf16[3,2,256,2,128]{4,3,1,0,2:T(2,128)(2,1)S(1)} async-done(((bf16[3,2,256,2,128]{4,3,1,0,2:T(2,128)(2,1)}), bf16[3,2,256,2,128]{4,3,1,0,2:T(2,128)(2,1)S(1)}, u32[]{:S(2)}, u32[]{:S(2)}) %all-to-all-start) | async-done | bytes 786464 | tf_op jit(solution)/shard_map/all_to_all | solution.py:49
  188.0 0.1 copy.34
  188.1 0.1 fusion.11
  188.2 0.3 copy.36
  188.5 0.3 copy.37
  188.7 0.3 copy.35
  189.0 0.3 fusion.4
  189.3 0.3 fusion.5
  189.6 0.2 copy.39
  189.9 15.6 %all_to_all.30 = bf16[16,32,2,128]{3,2,1,0:T(2,128)(2,1)S(1)} all-to-all(bf16[16,32,2,128]{3,2,1,0:T(2,128)(2,1)S(1)} %copy.39), channel_id=1, replica_groups={{0,16,32,48,64,80,96,112},{128,144,160,176,192,208,224,240},{256,272,28..., dimensions={0} | all-to-all | bytes 524288 | tf_op jit(solution)/shard_map/all_to_all | solution.py:53
  205.5 0.2 copy.40
  205.7 80.1 %all-gather.5.cloned.1.call-done = bf16[256,4096]{1,0:T(8,128)(2,1)} async-done(((bf16[256,128]{1,0:T(8,128)(2,1)}), bf16[256,4096]{1,0:T(8,128)(2,1)}) %all-gather.5.cloned.1.call-update) | async-done | bytes 2097168 | tf_op jit(solution)/shard_map/all_gather | solution.py:58
  285.8 4.8 %convolution_convert_fusion = bf16[512,4096]{1,0:T(8,128)(2,1)} fusion(bf16[256,4096]{1,0:T(8,128)(2,1)} %all-gather.5.cloned.1.call-done, bf16[64,8,2,128]{3,2,1,0:T(2,128)(2,1)S(1)} %bitcast.42), kind=kOutput, calls=%fused_computation.5 | convolution fusion | flops 1075838976 | bytes 6553600 | tf_op jit(solution)/shard_map/dot_general | solution.py:56
  290.6 0.0 reduce-scatter.2.cloned.1.call-update
  290.6 123.5 %reduce-scatter.2.cloned.1.call-done = bf16[512,256]{1,0:T(8,128)(2,1)} async-done(((bf16[512,4096]{1,0:T(8,128)(2,1)}), bf16[512,256]{1,0:T(8,128)(2,1)}) %reduce-scatter.2.cloned.1.call-update) | async-done | bytes 262160 | tf_op jit(solution)/shard_map/reduce_scatter | solution.py:61
  (6 shorter events, 0.0 us)
Async XLA Ops:
  6.5 5.8 %copy-start.2 = (f32[4096]{0:T(1024)S(1)}, f32[4096]{0:T(1024)}, u32[]{:S(2)}) copy-start(f32[4096]{0:T(1024)} %param.7) | copy-start | bytes 49156
  6.5 144.9 %all-gather.3.cloned.1.call-start = ((), (), s32[]{:S(2)}) async-start(), calls=%async_computation.3 | async-start | bytes 6488064 | tf_op jit(solution)/shard_map/all_gather | solution.py:41
  8.3 277.5 %all-gather.5.cloned.1.call-start = ((), (), s32[]{:S(2)}) async-start(), calls=%async_computation.4 | async-start | bytes 2162688 | tf_op jit(solution)/shard_map/all_gather | solution.py:58
  9.1 3.5 copy-start
  158.3 1.2 copy-start.1
  159.7 4.1 copy-start.3
  159.7 4.1 copy-start.4
  167.3 20.7 %all-to-all-start = ((bf16[3,2,256,2,128]{4,3,1,0,2:T(2,128)(2,1)}), bf16[3,2,256,2,128]{4,3,1,0,2:T(2,128)(2,1)S(1)}, u32[]{:S(2)}, u32[]{:S(2)}) async-start(bf16[3,2,256,2,128]{4,3,1,0,2:T(2,128)(2,1)} %pad_maximum_fusion), calls=%async_computation | async-start | bytes 1572864 | tf_op jit(solution)/shard_map/all_to_all | solution.py:49
  173.0 241.1 %reduce-scatter.2.cloned.1.call-start = ((), (), s32[]{:S(2)}) async-start(), calls=%async_computation.5 | async-start | bytes 4456448 | tf_op jit(solution)/shard_map/reduce_scatter | solution.py:61
Sparse Core Ops, SparseCore 0:
  9.4 142.0 all-gather.2
  153.4 132.3 all-gather.4
  290.8 123.3 reduce-scatter.1

commit v2 on v1

v2 whole, which is shorter than its diff:
```python
import functools

import jax
import jax.numpy as jnp
from jax import lax
from jax.experimental import pallas as pl
from jax.experimental.pallas import tpu as pltpu
from jax.sharding import PartitionSpec as P

MESH = pl.DeviceIdType.MESH
NY, NZ, NX = 4, 8, 4
WAVES = 2
HPW = 2 // WAVES
CW = 128 * HPW
HALF = NZ // 2


def wrap(value, size):
    return lax.rem(value + size, size)


def kernel(
    tok_hbm, gain_ref, qg_ref, kg_ref, wq_ref, wout_ref, out_ref,
    tok, wbuf, wo, nbuf, xall, acc, abuf, aall, oacc,
    tok_sem, ws_z, ws_y, wr, wr_half,
    os_z, os_y, os_swap, orecv, or_half,
    xs_a, xr_a, xs_g, xr_g,
    as_a, ar_a, as_g, ar_g,
):
    t = lax.axis_index("tm")
    j = lax.axis_index("tensor")
    y, z = t // NZ, t % NZ
    x, h, c = j // 4, (j // 2) % 2, j % 2

    def tm_dev(yy, zz):
        return (yy * NZ + zz, j)

    def tensor_id(xx, hh, cc):
        return (xx * 2 + hh) * 2 + cc

    def tensor_dev(xx, hh, cc):
        return (t, tensor_id(xx, hh, cc))

    def send(src, dst, ssem, rsem, device):
        pltpu.make_async_remote_copy(
            src_ref=src, dst_ref=dst, send_sem=ssem, recv_sem=rsem,
            device_id=device, device_id_type=MESH,
        ).start()

    def await_bytes(ref, sem):
        pltpu.make_async_copy(ref, ref, sem).wait()

    swap_t, swap_j = 2 * j + t % 2, t // 2
    swap_self = jnp.logical_and(swap_t == t, swap_j == j)
    swap_other = jnp.logical_not(swap_self)

    tok_copy = pltpu.make_async_copy(tok_hbm, tok, tok_sem)
    tok_copy.start()

    for w in range(WAVES):
        for i in range(3):
            wbuf[w, t, :, i * CW:(i + 1) * CW] = wq_ref[i, :, w * CW:(w + 1) * CW]

    barrier = pltpu.get_barrier_semaphore()
    partners = [tm_dev(y, wrap(z + d, NZ)) for d in range(1, NZ)]
    partners += [tm_dev(wrap(y + d, NY), z) for d in range(1, NY)]
    partners += [tensor_dev(wrap(x + d, NX), h, c) for d in range(1, NX)]
    partners += [tensor_dev(x, 1 - h, c), tensor_dev(x, h, 1 - c)]
    for device in partners:
        pl.semaphore_signal(barrier, inc=1, device_id=device, device_id_type=MESH)

    @pl.when(swap_other)
    def _():
        pl.semaphore_signal(barrier, inc=1, device_id=(swap_t, swap_j), device_id_type=MESH)

    pl.semaphore_wait(barrier, len(partners) + swap_other.astype(jnp.int32))

    right, left = tm_dev(y, wrap(z + 1, NZ)), tm_dev(y, wrap(z + NZ - 1, NZ))

    def row_of(d):
        return wrap(y + d, NY)

    def w_block(w, b, part):
        if part is None:
            return wbuf.at[w, b]
        return wbuf.at[w, b, pl.ds(part * 64, 64)]

    def w_send_y(w):
        for d in range(1, NY):
            send(wbuf.at[w, t], wbuf.at[w, t], ws_y.at[w, d], wr.at[w, t], tm_dev(wrap(y + d, NY), z))

    def w_first(w, d):
        b = row_of(d) * NZ + z
        for way, device in ((0, right), (1, left)):
            send(wbuf.at[w, b], wbuf.at[w, b], ws_z.at[w, d, 0, way], wr.at[w, b], device)

    def w_from_y(w):
        @pl.loop(1, NY)
        def _(d):
            b = row_of(d) * NZ + z
            await_bytes(wbuf.at[w, b], wr.at[w, b])
            w_first(w, d)

    def w_pair(d, k):
        base = row_of(d) * NZ
        return base + wrap(z - k, NZ), base + wrap(z + k, NZ)

    def w_forward(w, k, then=None):
        @pl.loop(0, NY)
        def _(d):
            for way, (b, device) in enumerate(zip(w_pair(d, k), (right, left))):
                await_bytes(wbuf.at[w, b], wr.at[w, b])
                if k < HALF - 1:
                    send(wbuf.at[w, b], wbuf.at[w, b], ws_z.at[w, d, k, way], wr.at[w, b], device)
                else:
                    piece = w_block(w, b, way)
                    rsem = wr.at[w, b] if way == 0 else wr_half.at[w, row_of(d)]
                    send(piece, piece, ws_z.at[w, d, k, way], rsem, device)
            if then is not None:
                then(d)

    def w_last(w, d):
        b, _ = w_pair(d, HALF)
        await_bytes(w_block(w, b, 0), wr.at[w, b])
        await_bytes(w_block(w, b, 1), wr_half.at[w, row_of(d)])

    def multiply(w, blocks):
        @pl.loop(0, 2)
        def _(r):
            total = acc[w, pl.ds(r * 8, 8)].reshape(256, 3 * CW)
            for b in blocks:
                rows = xall[b // 2, pl.ds(r * 256, 256), pl.ds(pl.multiple_of((b % 2) * 128, 128), 128)]
                total = total + jnp.dot(rows, wbuf[w, b], preferred_element_type=jnp.float32)
            acc[w, pl.ds(r * 8, 8)] = total.reshape(8, 32, 3 * CW)

    def multiply_first(w):
        @pl.loop(0, NY // 2)
        def _(d):
            multiply(w, [row_of(2 * d) * NZ + z, row_of(2 * d + 1) * NZ + z])

    def multiply_pair(w, k):
        @pl.loop(0, NY)
        def _(d):
            multiply(w, w_pair(d, k))

    def multiply_last(w):
        @pl.loop(0, NY)
        def _(d):
            w_last(w, d)
            multiply(w, [w_pair(d, HALF)[0]])

    def o_spread(b, n):
        for d in range(1, NY):
            send(wo.at[b], wo.at[b], os_y.at[n, d], orecv.at[b], tm_dev(wrap(y + d, NY), z))

    def o_first():
        @pl.when(swap_other)
        def _():
            await_bytes(wo.at[t], orecv.at[t])

        for way, device in ((0, right), (1, left)):
            send(wo.at[t], wo.at[t], os_z.at[0, way], orecv.at[t], device)
        o_spread(t, 0)

    def o_forward(k):
        for way, (b, device) in enumerate(((y * NZ + wrap(z - k, NZ), right), (y * NZ + wrap(z + k, NZ), left))):
            await_bytes(wo.at[b], orecv.at[b])
            if k < HALF - 1:
                send(wo.at[b], wo.at[b], os_z.at[k, way], orecv.at[b], device)
            else:
                piece = wo.at[b, pl.ds(way * 128, 128)]
                rsem = orecv.at[b] if way == 0 else or_half.at[0]
                send(piece, piece, os_z.at[k, way], rsem, device)
            o_spread(b, 2 * k - 1 + way)

    def o_last():
        b = y * NZ + wrap(z + HALF, NZ)
        await_bytes(wo.at[b, pl.ds(0, 128)], orecv.at[b])
        await_bytes(wo.at[b, pl.ds(128, 128)], or_half.at[0])
        o_spread(b, 7)

    def o_all():
        @pl.loop(1, NY)
        def _(d):
            for zz in range(NZ):
                b = row_of(d) * NZ + zz
                await_bytes(wo.at[b], orecv.at[b])

    def near(first, block, index, ssem, rsem):
        devices = [tensor_dev(x, h, 1 - c)]
        if first:
            devices.append(tensor_dev(x, 1 - h, c))
        devices += [tensor_dev(wrap(x + d, NX), h, c) for d in range(1, NX)]
        for n, device in enumerate(devices):
            send(block(index), block(index), ssem(n if first else 5 + n), rsem(index), device)

    def gather_own(block, ssem, rsem):
        near(True, block, j, ssem, rsem)

    def gather_partner(block, ssem, rsem):
        other = tensor_id(x, 1 - h, c)
        await_bytes(block(other), rsem(other))
        near(False, block, other, ssem, rsem)

    def gather_x(block, ssem, rsem):
        n = 9
        for hh in (h, 1 - h):
            for d in (1, 3, 2):
                other = tensor_id(wrap(x + d, NX), hh, c)
                await_bytes(block(other), rsem(other))
                send(block(other), block(other), ssem(n), rsem(other), tensor_dev(x, h, 1 - c))
                n += 1

    def gather_sibling(block, rsem):
        @pl.loop(0, 8)
        def _(n):
            other = n * 2 + 1 - c
            await_bytes(block(other), rsem(other))

    def x_block(index):
        return xall.at[index]

    def x_ss(n):
        return xs_g.at[n]

    def x_rs(index):
        return xr_g.at[index]

    def a_tools(w):
        return (
            lambda index: aall.at[w, index],
            lambda n: as_g.at[w, n],
            lambda index: ar_g.at[w, index],
        )

    def attention(w):
        shape = (256, 256)
        fr = lax.broadcasted_iota(jnp.int32, shape, 0)
        gc = lax.broadcasted_iota(jnp.int32, shape, 1)
        mask = jnp.logical_and((fr & 15) == (gc & 15), (gc >> 4) <= (fr >> 4))
        for hd in range(HPW):
            for ph in range(2):
                def part(i):
                    lo = i * CW + hd * 128
                    return acc[w, :, ph * 16:(ph + 1) * 16, lo:lo + 128].reshape(256, 128)

                def normed(i, gains):
                    raw = part(i)
                    scale = lax.rsqrt(jnp.mean(raw * raw, axis=-1, keepdims=True) + 1e-06)
                    head = w * HPW + hd
                    return (raw * scale * gains[head:head + 1, :]).astype(jnp.bfloat16)

                query, key = normed(0, qg_ref), normed(1, kg_ref)
                value = part(2).astype(jnp.bfloat16)
                scores = lax.dot_general(
                    query, key, (((1,), (1,)), ((), ())), preferred_element_type=jnp.float32
                ) / jnp.sqrt(jnp.float32(128))
                expo = jnp.where(mask, jnp.exp(scores), jnp.float32(0.0))
                weights = (expo / jnp.sum(expo, axis=-1, keepdims=True)).astype(jnp.bfloat16)
                att = jnp.dot(weights, value, preferred_element_type=jnp.float32).astype(jnp.bfloat16)
                abuf[w, :, ph * 16:(ph + 1) * 16, hd * 128:(hd + 1) * 128] = att.reshape(16, 16, 128)
        aall[w, j, pl.ds(z * 64, 64)] = abuf[w, pl.ds(2 * z, 2)].reshape(64, CW)
        for d in range(1, NZ):
            zz = wrap(z + d, NZ)
            send(
                abuf_flat(w, zz), aall.at[w, j, pl.ds(z * 64, 64)],
                as_a.at[w, d], ar_a.at[w, z], tm_dev(y, zz),
            )

    def abuf_flat(w, zz):
        return abuf.at[w, pl.ds(2 * zz, 2)].reshape(64, CW)

    def a_pieces(w):
        for d in range(1, NZ):
            zz = wrap(z + d, NZ)
            await_bytes(aall.at[w, j, pl.ds(zz * 64, 64)], ar_a.at[w, zz])

    def project(w, index):
        lo = w * CW
        rhs = jnp.concatenate([wo[2 * index, lo:lo + CW, :], wo[2 * index + 1, lo:lo + CW, :]], axis=-1)

        @pl.loop(0, 2)
        def _(r):
            rows = pl.ds(r * 256, 256)
            oacc[rows] = oacc[rows] + jnp.dot(
                aall[w, index, rows], rhs, preferred_element_type=jnp.float32
            )

    w_send_y(0)
    w_first(0, 0)

    @pl.when(swap_other)
    def _():
        send(wout_ref, wo.at[swap_t], os_swap.at[0], orecv.at[swap_t], (swap_t, swap_j))

    @pl.when(swap_self)
    def _():
        wo[t] = wout_ref[...]

    acc[...] = jnp.zeros_like(acc)
    oacc[...] = jnp.zeros_like(oacc)

    tok_copy.wait()
    columns = pl.ds(pl.multiple_of(j * 256, 256), 256)
    gain = gain_ref[:, columns]

    @pl.loop(0, 16)
    def _(n):
        rows = pl.ds(pl.multiple_of(n * 32, 32), 32)
        values = tok[rows].astype(jnp.float32)
        meansq = jnp.mean(values * values, axis=-1, keepdims=True)
        mine = tok[rows, columns].astype(jnp.float32)
        piece = (mine * lax.rsqrt(meansq + 1e-06) * gain).astype(jnp.bfloat16)
        nbuf[n % 8, pl.ds(pl.multiple_of((n // 8) * 32, 32), 32)] = piece

    xall[j, pl.ds(z * 64, 64)] = nbuf[z]
    for d in range(1, NZ):
        zz = wrap(z + d, NZ)
        send(nbuf.at[zz], xall.at[j, pl.ds(z * 64, 64)], xs_a.at[d], xr_a.at[z], tm_dev(y, zz))

    w_from_y(0)
    o_first()

    for d in range(1, NZ):
        zz = wrap(z + d, NZ)
        await_bytes(xall.at[j, pl.ds(zz * 64, 64)], xr_a.at[zz])
    gather_own(x_block, x_ss, x_rs)

    w_forward(0, 1)
    o_forward(1)
    gather_partner(x_block, x_ss, x_rs)
    w_forward(0, 2)
    o_forward(2)
    if WAVES > 1:
        w_send_y(1)
        w_first(1, 0)
    gather_x(x_block, x_ss, x_rs)
    w_forward(0, 3)
    o_forward(3)
    if WAVES > 1:
        w_from_y(1)
    gather_sibling(x_block, x_rs)

    multiply_first(0)
    multiply_pair(0, 1)
    if WAVES > 1:
        w_forward(1, 1)
    o_last()
    multiply_pair(0, 2)
    multiply_pair(0, 3)
    if WAVES > 1:
        w_forward(1, 2)
    multiply_last(0)
    attention(0)

    if WAVES > 1:
        w_forward(1, 3)
        multiply_first(1)
        multiply_pair(1, 1)
        a_pieces(0)
        gather_own(*a_tools(0))
        multiply_pair(1, 2)
        multiply_pair(1, 3)
        gather_partner(*a_tools(0))
        multiply_last(1)
        attention(1)
        gather_x(*a_tools(0))
        o_all()
        block, ss, rs = a_tools(0)
        gather_sibling(block, rs)
        a_pieces(1)
        gather_own(*a_tools(1))

        @pl.loop(0, 16)
        def _(n):
            project(0, n)

        gather_partner(*a_tools(1))
    else:
        a_pieces(0)
        gather_own(*a_tools(0))
        gather_partner(*a_tools(0))
        o_all()

    w = WAVES - 1
    block, ss, rs = a_tools(w)
    project(w, j)
    project(w, tensor_id(x, 1 - h, c))
    gather_x(block, ss, rs)
    for hh in (h, 1 - h):
        for d in (1, 3, 2):
            project(w, tensor_id(wrap(x + d, NX), hh, c))

    @pl.loop(0, 8)
    def _(n):
        other = n * 2 + 1 - c
        await_bytes(block(other), rs(other))
        project(w, other)

    for n in range(NZ):
        part = oacc[n * 64:(n + 1) * 64].astype(jnp.bfloat16).reshape(2, 32, 256)
        out_ref[:, n * 32:(n + 1) * 32, :] = part

    for w in range(WAVES):
        for d in range(1, NY):
            await_bytes(wbuf.at[w, t], ws_y.at[w, d])

        @pl.loop(0, NY)
        def _(d):
            for way in range(2):
                for k in range(HALF - 1):
                    await_bytes(wbuf.at[w, t], ws_z.at[w, d, k, way])
                await_bytes(w_block(w, t, 0), ws_z.at[w, d, HALF - 1, way])

        for d in range(1, NZ):
            await_bytes(abuf_flat(w, z), as_a.at[w, d])

        @pl.loop(0, 15)
        def _(n):
            await_bytes(aall.at[w, 0], as_g.at[w, n])

    for way in range(2):
        for k in range(HALF - 1):
            await_bytes(wo.at[0], os_z.at[k, way])
        await_bytes(wo.at[0, pl.ds(0, 128)], os_z.at[HALF - 1, way])

    @pl.loop(0, 8)
    def _(n):
        for d in range(1, NY):
            await_bytes(wo.at[0], os_y.at[n, d])

    @pl.when(swap_other)
    def _():
        await_bytes(wout_ref, os_swap.at[0])

    for d in range(1, NZ):
        await_bytes(nbuf.at[0], xs_a.at[d])

    @pl.loop(0, 15)
    def _(n):
        await_bytes(xall.at[0], xs_g.at[n])


def body(tokens, norm_gain, q_gain, k_gain, w_qkv, w_out):
    frames_dev, patches, width = tokens.shape
    count = frames_dev * patches
    vmem = pl.BlockSpec(memory_space=pltpu.VMEM)
    dma = pltpu.SemaphoreType.DMA
    bf16, f32 = jnp.bfloat16, jnp.float32
    return pl.pallas_call(
        kernel,
        out_shape=jax.ShapeDtypeStruct((frames_dev, patches, 256), bf16),
        in_specs=[pl.BlockSpec(memory_space=pl.ANY)] + [vmem] * 5,
        out_specs=vmem,
        scratch_shapes=[
            pltpu.VMEM((count, width), bf16),
            pltpu.VMEM((WAVES, NY * NZ, 128, 3 * CW), bf16),
            pltpu.VMEM((NY * NZ, 256, 128), bf16),
            pltpu.VMEM((NZ, 64, 256), bf16),
            pltpu.VMEM((16, count, 256), bf16),
            pltpu.VMEM((WAVES, 16, 32, 3 * CW), f32),
            pltpu.VMEM((WAVES, 16, 32, CW), bf16),
            pltpu.VMEM((WAVES, 16, count, CW), bf16),
            pltpu.VMEM((count, 256), f32),
            dma, dma((WAVES, NY, HALF, 2)), dma((WAVES, NY)), dma((WAVES, NY * NZ)), dma((WAVES, NY)),
            dma((HALF, 2)), dma((8, NY)), dma((1,)), dma((NY * NZ,)), dma((1,)),
            dma((NZ,)), dma((NZ,)), dma((15,)), dma((16,)),
            dma((WAVES, NZ)), dma((WAVES, NZ)), dma((WAVES, 15)), dma((WAVES, 16)),
        ],
        compiler_params=pltpu.CompilerParams(
            collective_id=0, has_side_effects=True, vmem_limit_bytes=56 * 1024 * 1024
        ),
        cost_estimate=pl.CostEstimate(
            flops=2 * count * width * 1024, bytes_accessed=16 * 1024 * 1024, transcendentals=count * 1024
        ),
    )(
        tokens.reshape(count, width), norm_gain.reshape(1, width), q_gain, k_gain, w_qkv, w_out
    )


def solution(mesh):
    placed = (
        P("tm", None, None),
        P(),
        P("tensor", None),
        P("tensor", None),
        P(None, "tm", "tensor"),
        P("tensor", "tm"),
    )
    return jax.shard_map(
        body, mesh=mesh, in_specs=placed, out_specs=P("tm", None, "tensor"), check_vma=False
    )
```

time: 421 us -> 161 us (0.38)
  the two profiles are of different devices: /device:TPU:1 before, /device:TPU:13 now
where the time goes in v2:
time: 161 us
  Pallas kernels  160 us (99%)
  local copies, waits for them, and re-layouts  1.67 us (1%)
    pallas_call x1, Pallas kernels, body(): pl.pallas_call(kernel, out_shape=jax.ShapeDtypeStruct((frames_dev, patche...  160 us

profile of v2, /device:TPU:13, one launch (start us, length us, event | category | flops | bytes accessed | tf_op | source)
XLA Modules:
  0.0 161.2 jit_solution(6803758514400061881)
XLA Ops:
  0.0 159.6 %shard_map.64 = bf16[2,256,256]{2,1,0:T(8,128)(2,1)} custom-call(bf16[512,4096]{1,0:T(8,128)(2,1)} %bitcast.2, f32[1,4096]{1,0:T(1,128)} %bitcast.3, f32[2,128]{1,0:T(2,128)} %qg_ref.1, f32[2,128]{1,0:T(2,128)} %kg_ref.1, bf16[3,128,256]{2,1,0:T(8,128)(2,1)} %wq_ref.1, bf16[256,128]{1,0:T(8,128)(2,1)} %wout_ref.1), custom_call_target="tpu_custom_call" | custom-call | flops 4294967296 | bytes 16777216 | tf_op jit(solution)/shard_map/pallas_call | solution.py:450
  159.6 1.7 %copy.8 = bf16[2,256,256]{2,1,0:T(8,128)(2,1)} copy(bf16[2,256,256]{2,1,0:T(8,128)(2,1)} %shard_map.64) | data formatting | bytes 524288

commit v3 on v2

v3 whole, which is shorter than its diff:
```python
import functools

import jax
import jax.numpy as jnp
from jax import lax
from jax.experimental import pallas as pl
from jax.experimental.pallas import tpu as pltpu
from jax.sharding import PartitionSpec as P

MESH = pl.DeviceIdType.MESH
NY, NZ, NX = 4, 8, 4
WAVES = 2
HPW = 2 // WAVES
CW = 128 * HPW
HALF = NZ // 2


def wrap(value, size):
    return lax.rem(value + size, size)


def kernel(
    tok_hbm, gain_ref, qg_ref, kg_ref, wq_ref, wout_ref, out_ref,
    tok, wbuf, wo, nbuf, xall, acc, abuf, aall, oacc,
    tok_sem, ws_z, ws_y, wr, wr_half,
    os_z, os_y, os_swap, orecv, or_half,
    xs_a, xr_a, xs_g, xr_g,
    as_a, ar_a, as_g, ar_g,
):
    t = lax.axis_index("tm")
    j = lax.axis_index("tensor")
    y, z = t // NZ, t % NZ
    x, h, c = j // 4, (j // 2) % 2, j % 2

    def tm_dev(yy, zz):
        return (yy * NZ + zz, j)

    def tensor_id(xx, hh, cc):
        return (xx * 2 + hh) * 2 + cc

    def tensor_dev(xx, hh, cc):
        return (t, tensor_id(xx, hh, cc))

    def send(src, dst, ssem, rsem, device):
        pltpu.make_async_remote_copy(
            src_ref=src, dst_ref=dst, send_sem=ssem, recv_sem=rsem,
            device_id=device, device_id_type=MESH,
        ).start()

    def await_bytes(ref, sem):
        pltpu.make_async_copy(ref, ref, sem).wait()

    swap_t, swap_j = 2 * j + t % 2, t // 2
    swap_self = jnp.logical_and(swap_t == t, swap_j == j)
    swap_other = jnp.logical_not(swap_self)

    tok_copy = pltpu.make_async_copy(tok_hbm, tok, tok_sem)
    tok_copy.start()

    for w in range(WAVES):
        for i in range(3):
            wbuf[w, t, :, i * CW:(i + 1) * CW] = wq_ref[i, :, w * CW:(w + 1) * CW]

    barrier = pltpu.get_barrier_semaphore()
    partners = [tm_dev(y, wrap(z + d, NZ)) for d in range(1, NZ)]
    partners += [tm_dev(wrap(y + d, NY), z) for d in range(1, NY)]
    partners += [tensor_dev(wrap(x + d, NX), h, c) for d in range(1, NX)]
    partners += [tensor_dev(x, 1 - h, c), tensor_dev(x, h, 1 - c)]
    for device in partners:
        pl.semaphore_signal(barrier, inc=1, device_id=device, device_id_type=MESH)

    @pl.when(swap_other)
    def _():
        pl.semaphore_signal(barrier, inc=1, device_id=(swap_t, swap_j), device_id_type=MESH)

    pl.semaphore_wait(barrier, len(partners) + swap_other.astype(jnp.int32))

    right, left = tm_dev(y, wrap(z + 1, NZ)), tm_dev(y, wrap(z + NZ - 1, NZ))

    def row_of(d):
        return wrap(y + d, NY)

    def ring_pair(d, k):
        base = row_of(d) * NZ
        return base + wrap(z - k, NZ), base + wrap(z + k, NZ)

    def ring_tools(block, half, ss_y, ss_z, rs, rs_half):
        def send_y():
            for d in range(1, NY):
                send(block(t), block(t), ss_y(d), rs(t), tm_dev(wrap(y + d, NY), z))

        def first(d):
            b = row_of(d) * NZ + z
            for way, device in ((0, right), (1, left)):
                send(block(b), block(b), ss_z(d, 0, way), rs(b), device)

        def from_y():
            @pl.loop(1, NY)
            def _(d):
                b = row_of(d) * NZ + z
                await_bytes(block(b), rs(b))
                first(d)

        def forward(k):
            @pl.loop(0, NY)
            def _(d):
                for way, (b, device) in enumerate(zip(ring_pair(d, k), (right, left))):
                    await_bytes(block(b), rs(b))
                    if k < HALF - 1:
                        send(block(b), block(b), ss_z(d, k, way), rs(b), device)
                    else:
                        rsem = rs(b) if way == 0 else rs_half(row_of(d))
                        send(half(b, way), half(b, way), ss_z(d, k, way), rsem, device)

        def last(d):
            b, _ = ring_pair(d, HALF)
            await_bytes(half(b, 0), rs(b))
            await_bytes(half(b, 1), rs_half(row_of(d)))

        def sent():
            for d in range(1, NY):
                await_bytes(block(t), ss_y(d))

            @pl.loop(0, NY)
            def _(d):
                for way in range(2):
                    for k in range(HALF - 1):
                        await_bytes(block(t), ss_z(d, k, way))
                    await_bytes(half(t, 0), ss_z(d, HALF - 1, way))

        return send_y, first, from_y, forward, last, sent

    def w_tools(w):
        return ring_tools(
            lambda b: wbuf.at[w, b], lambda b, way: wbuf.at[w, b, pl.ds(way * 64, 64)],
            lambda d: ws_y.at[w, d], lambda d, k, way: ws_z.at[w, d, k, way],
            lambda b: wr.at[w, b], lambda row: wr_half.at[w, row],
        )

    w_send_y, w_first, w_from_y, w_forward, w_last, w_sent = zip(*[w_tools(w) for w in range(WAVES)])

    def o_at(b):
        return pl.ds(pl.multiple_of((b // 2) * 128, 128), 128), pl.ds(pl.multiple_of((b % 2) * 128, 128), 128)

    def o_block(b):
        return wo.at[(slice(None), *o_at(b))]

    def o_half(b, way):
        return wo.at[(way, *o_at(b))]

    def o_spread(b, n):
        for d in range(1, NY):
            send(o_block(b), o_block(b), os_y.at[n, d], orecv.at[b], tm_dev(wrap(y + d, NY), z))

    def o_first():
        @pl.when(swap_other)
        def _():
            await_bytes(o_block(t), orecv.at[t])

        for way, device in ((0, right), (1, left)):
            send(o_block(t), o_block(t), os_z.at[0, way], orecv.at[t], device)
        o_spread(t, 0)

    def o_forward(k):
        for way, (b, device) in enumerate(zip(ring_pair(0, k), (right, left))):
            await_bytes(o_block(b), orecv.at[b])
            if k < HALF - 1:
                send(o_block(b), o_block(b), os_z.at[k, way], orecv.at[b], device)
            else:
                rsem = orecv.at[b] if way == 0 else or_half.at[0]
                send(o_half(b, way), o_half(b, way), os_z.at[k, way], rsem, device)
            o_spread(b, 2 * k - 1 + way)

    def o_last():
        b, _ = ring_pair(0, HALF)
        await_bytes(o_half(b, 0), orecv.at[b])
        await_bytes(o_half(b, 1), or_half.at[0])
        o_spread(b, 7)

    def o_all():
        @pl.loop(1, NY)
        def _(d):
            for zz in range(NZ):
                b = row_of(d) * NZ + zz
                await_bytes(o_block(b), orecv.at[b])

    def o_sent():
        for way in range(2):
            for k in range(HALF - 1):
                await_bytes(o_block(t), os_z.at[k, way])
            await_bytes(o_half(t, 0), os_z.at[HALF - 1, way])

        @pl.loop(0, NZ)
        def _(n):
            for d in range(1, NY):
                await_bytes(o_block(t), os_y.at[n, d])

    def multiply(w):
        @pl.loop(0, NY)
        def _(d):
            w_last[w](d)
            row = row_of(d)
            depth = NZ * 128

            @pl.loop(0, 2)
            def _(r):
                total = jnp.dot(
                    xall[pl.ds(pl.multiple_of(r * 256, 256), 256), pl.ds(pl.multiple_of(row * depth, depth), depth)],
                    wbuf[w, pl.ds(row * NZ, NZ)].reshape(depth, 3 * CW),
                    preferred_element_type=jnp.float32,
                )
                acc[w, pl.ds(r * 8, 8)] = acc[w, pl.ds(r * 8, 8)] + total.reshape(8, 32, 3 * CW)

    def near(first, block, index, ssem, rsem):
        devices = [tensor_dev(x, h, 1 - c)]
        if first:
            devices.append(tensor_dev(x, 1 - h, c))
        devices += [tensor_dev(wrap(x + d, NX), h, c) for d in range(1, NX)]
        for n, device in enumerate(devices):
            send(block(index), block(index), ssem(n if first else 5 + n), rsem(index), device)

    def gather_own(block, ssem, rsem):
        near(True, block, j, ssem, rsem)

    def gather_partner(block, ssem, rsem):
        other = tensor_id(x, 1 - h, c)
        await_bytes(block(other), rsem(other))
        near(False, block, other, ssem, rsem)

    def gather_x(block, ssem, rsem):
        n = 9
        for hh in (h, 1 - h):
            for d in (1, 3, 2):
                other = tensor_id(wrap(x + d, NX), hh, c)
                await_bytes(block(other), rsem(other))
                send(block(other), block(other), ssem(n), rsem(other), tensor_dev(x, h, 1 - c))
                n += 1

    def gather_sibling(block, rsem):
        @pl.loop(0, 8)
        def _(n):
            other = n * 2 + 1 - c
            await_bytes(block(other), rsem(other))

    def x_rows(index, start, size):
        return xall.at[pl.ds(start, size), pl.ds(pl.multiple_of(index * 256, 256), 256)]

    def x_pieces():
        for d in range(1, NZ):
            zz = wrap(z + d, NZ)
            await_bytes(x_rows(j, zz * 64, 64), xr_a.at[zz])

    def x_block(index):
        return x_rows(index, 0, 512)

    def x_ss(n):
        return xs_g.at[n]

    def x_rs(index):
        return xr_g.at[index]

    def a_rows(w, index, start, size):
        return aall.at[w, pl.ds(start, size), pl.ds(pl.multiple_of(index * CW, CW), CW)]

    def a_tools(w):
        return (
            lambda index: a_rows(w, index, 0, 512),
            lambda n: as_g.at[w, n],
            lambda index: ar_g.at[w, index],
        )

    def attention(w):
        shape = (256, 256)
        fr = lax.broadcasted_iota(jnp.int32, shape, 0)
        gc = lax.broadcasted_iota(jnp.int32, shape, 1)
        mask = jnp.logical_and((fr & 15) == (gc & 15), (gc >> 4) <= (fr >> 4))
        for hd in range(HPW):
            for ph in range(2):
                def part(i):
                    lo = i * CW + hd * 128
                    return acc[w, :, ph * 16:(ph + 1) * 16, lo:lo + 128].reshape(256, 128)

                def normed(i, gains):
                    raw = part(i)
                    scale = lax.rsqrt(jnp.mean(raw * raw, axis=-1, keepdims=True) + 1e-06)
                    head = w * HPW + hd
                    return (raw * scale * gains[head:head + 1, :]).astype(jnp.bfloat16)

                query, key = normed(0, qg_ref), normed(1, kg_ref)
                value = part(2).astype(jnp.bfloat16)
                scores = lax.dot_general(
                    query, key, (((1,), (1,)), ((), ())), preferred_element_type=jnp.float32
                ) / jnp.sqrt(jnp.float32(128))
                expo = jnp.where(mask, jnp.exp(scores), jnp.float32(0.0))
                weights = (expo / jnp.sum(expo, axis=-1, keepdims=True)).astype(jnp.bfloat16)
                att = jnp.dot(weights, value, preferred_element_type=jnp.float32).astype(jnp.bfloat16)
                abuf[w, :, ph * 16:(ph + 1) * 16, hd * 128:(hd + 1) * 128] = att.reshape(16, 16, 128)
        aall[w, pl.ds(z * 64, 64), pl.ds(pl.multiple_of(j * CW, CW), CW)] = abuf[w, pl.ds(2 * z, 2)].reshape(64, CW)
        for d in range(1, NZ):
            zz = wrap(z + d, NZ)
            send(
                abuf_flat(w, zz), a_rows(w, j, z * 64, 64),
                as_a.at[w, d], ar_a.at[w, z], tm_dev(y, zz),
            )

    def abuf_flat(w, zz):
        return abuf.at[w, pl.ds(2 * zz, 2)].reshape(64, CW)

    def a_pieces(w):
        for d in range(1, NZ):
            zz = wrap(z + d, NZ)
            await_bytes(a_rows(w, j, zz * 64, 64), ar_a.at[w, zz])

    def project(w):
        @pl.loop(0, 2)
        def _(r):
            rows = pl.ds(pl.multiple_of(r * 256, 256), 256)
            total = jnp.dot(aall[w, rows, :], wo[w], preferred_element_type=jnp.float32)
            if w > 0:
                total = oacc[rows] + total
            oacc[rows] = total

    w_send_y[0]()
    w_first[0](0)
    w_first[1](0)

    @pl.when(swap_other)
    def _():
        send(wout_ref, o_block(swap_t), os_swap.at[0], orecv.at[swap_t], (swap_t, swap_j))

    @pl.when(swap_self)
    def _():
        wo[(slice(None), *o_at(t))] = wout_ref[...]

    acc[...] = jnp.zeros_like(acc)

    tok_copy.wait()
    columns = pl.ds(pl.multiple_of(j * 256, 256), 256)
    gain = gain_ref[:, columns]

    @pl.loop(0, 16)
    def _(n):
        rows = pl.ds(pl.multiple_of(n * 32, 32), 32)
        values = tok[rows].astype(jnp.float32)
        meansq = jnp.mean(values * values, axis=-1, keepdims=True)
        mine = tok[rows, columns].astype(jnp.float32)
        piece = (mine * lax.rsqrt(meansq + 1e-06) * gain).astype(jnp.bfloat16)
        nbuf[n % 8, pl.ds(pl.multiple_of((n // 8) * 32, 32), 32)] = piece

    xall[pl.ds(z * 64, 64), columns] = nbuf[z]
    for d in range(1, NZ):
        zz = wrap(z + d, NZ)
        send(nbuf.at[zz], x_rows(j, z * 64, 64), xs_a.at[d], xr_a.at[z], tm_dev(y, zz))

    w_from_y[0]()
    x_pieces()
    gather_own(x_block, x_ss, x_rs)
    w_forward[0](1)
    w_send_y[1]()
    w_forward[0](2)
    gather_partner(x_block, x_ss, x_rs)
    o_first()
    w_forward[0](3)
    w_from_y[1]()
    o_forward(1)
    gather_x(x_block, x_ss, x_rs)
    w_forward[1](1)
    gather_sibling(x_block, x_rs)
    o_forward(2)
    multiply(0)
    attention(0)
    w_forward[1](2)
    o_forward(3)
    a_pieces(0)
    gather_own(*a_tools(0))
    w_forward[1](3)
    o_last()
    gather_partner(*a_tools(0))
    multiply(1)
    attention(1)
    gather_x(*a_tools(0))
    a_pieces(1)
    gather_own(*a_tools(1))
    gather_sibling(a_tools(0)[0], a_tools(0)[2])
    o_all()
    project(0)
    gather_partner(*a_tools(1))
    gather_x(*a_tools(1))
    gather_sibling(a_tools(1)[0], a_tools(1)[2])
    project(1)

    for n in range(NZ):
        part = oacc[n * 64:(n + 1) * 64].astype(jnp.bfloat16).reshape(2, 32, 256)
        out_ref[:, n * 32:(n + 1) * 32, :] = part

    for w in range(WAVES):
        w_sent[w]()

        for d in range(1, NZ):
            await_bytes(abuf_flat(w, z), as_a.at[w, d])

        @pl.loop(0, 15)
        def _(n):
            await_bytes(a_rows(w, 0, 0, 512), as_g.at[w, n])

    o_sent()

    @pl.when(swap_other)
    def _():
        await_bytes(wout_ref, os_swap.at[0])

    for d in range(1, NZ):
        await_bytes(nbuf.at[0], xs_a.at[d])

    @pl.loop(0, 15)
    def _(n):
        await_bytes(x_rows(0, 0, 512), xs_g.at[n])


def body(tokens, norm_gain, q_gain, k_gain, w_qkv, w_out):
    frames_dev, patches, width = tokens.shape
    count = frames_dev * patches
    vmem = pl.BlockSpec(memory_space=pltpu.VMEM)
    dma = pltpu.SemaphoreType.DMA
    bf16, f32 = jnp.bfloat16, jnp.float32
    return pl.pallas_call(
        kernel,
        out_shape=jax.ShapeDtypeStruct((frames_dev, patches, 256), bf16),
        in_specs=[pl.BlockSpec(memory_space=pl.ANY)] + [vmem] * 5,
        out_specs=vmem,
        scratch_shapes=[
            pltpu.VMEM((count, width), bf16),
            pltpu.VMEM((WAVES, NY * NZ, 128, 3 * CW), bf16),
            pltpu.VMEM((2, 2048, 256), bf16),
            pltpu.VMEM((NZ, 64, 256), bf16),
            pltpu.VMEM((count, width), bf16),
            pltpu.VMEM((WAVES, 16, 32, 3 * CW), f32),
            pltpu.VMEM((WAVES, 16, 32, CW), bf16),
            pltpu.VMEM((WAVES, count, 16 * CW), bf16),
            pltpu.VMEM((count, 256), f32),
            dma, dma((WAVES, NY, HALF, 2)), dma((WAVES, NY)), dma((WAVES, NY * NZ)), dma((WAVES, NY)),
            dma((HALF, 2)), dma((NZ, NY)), dma((1,)), dma((NY * NZ,)), dma((1,)),
            dma((NZ,)), dma((NZ,)), dma((15,)), dma((16,)),
            dma((WAVES, NZ)), dma((WAVES, NZ)), dma((WAVES, 15)), dma((WAVES, 16)),
        ],
        compiler_params=pltpu.CompilerParams(
            collective_id=0, has_side_effects=True, vmem_limit_bytes=56 * 1024 * 1024
        ),
        cost_estimate=pl.CostEstimate(
            flops=2 * count * width * 1024, bytes_accessed=16 * 1024 * 1024, transcendentals=count * 1024
        ),
    )(
        tokens.reshape(count, width), norm_gain.reshape(1, width), q_gain, k_gain, w_qkv, w_out.reshape(2, 128, 128)
    )


def solution(mesh):
    placed = (
        P("tm", None, None),
        P(),
        P("tensor", None),
        P("tensor", None),
        P(None, "tm", "tensor"),
        P("tensor", "tm"),
    )
    return jax.shard_map(
        body, mesh=mesh, in_specs=placed, out_specs=P("tm", None, "tensor"), check_vma=False
    )
```

time: 161 us -> 131 us (0.81)
  the two profiles are of different devices: /device:TPU:13 before, /device:TPU:1 now
where the time goes in v3:
time: 131 us; the launch traced here: 129 us
  Pallas kernels  128 us (98%)
  local copies, waits for them, and re-layouts  1.67 us (1%)
    pallas_call x1, Pallas kernels, body(): pl.pallas_call(kernel, out_shape=jax.ShapeDtypeStruct((frames_dev, patche...  128 us

profile of v3, /device:TPU:1, one launch (start us, length us, event | category | flops | bytes accessed | tf_op | source)
XLA Modules:
  0.0 129.4 jit_solution(16029825062810728668)
XLA Ops:
  0.0 127.7 %shard_map.64 = bf16[2,256,256]{2,1,0:T(8,128)(2,1)} custom-call(bf16[512,4096]{1,0:T(8,128)(2,1)} %bitcast.3, f32[1,4096]{1,0:T(1,128)} %bitcast.5, f32[2,128]{1,0:T(2,128)} %qg_ref.1, f32[2,128]{1,0:T(2,128)} %kg_ref.1, bf16[3,128,256]{2,1,0:T(8,128)(2,1)} %wq_ref.1, bf16[2,128,128]{2,1,0:T(8,128)(2,1)} %bitcast.4), custom_call_target="tpu_custom_call" | custom-call | flops 4294967296 | bytes 16777216 | tf_op jit(solution)/shard_map/pallas_call | solution.py:426
  127.7 1.7 %copy.8 = bf16[2,256,256]{2,1,0:T(8,128)(2,1)} copy(bf16[2,256,256]{2,1,0:T(8,128)(2,1)} %shard_map.64) | data formatting | bytes 524288

commit v4 on v3

--- a/solution.py
+++ b/solution.py
@@ -13,6 +13,7 @@
 HPW = 2 // WAVES
 CW = 128 * HPW
 HALF = NZ // 2
+SPLIT = 32
 
 
 def wrap(value, size):
@@ -22,7 +23,7 @@
 def kernel(
     tok_hbm, gain_ref, qg_ref, kg_ref, wq_ref, wout_ref, out_ref,
     tok, wbuf, wo, nbuf, xall, acc, abuf, aall, oacc,
-    tok_sem, ws_z, ws_y, wr, wr_half,
+    tok_sem, ws_z, ws_y, wr, wr_half, vs_z, vs_y, vr, vr_half,
     os_z, os_y, os_swap, orecv, or_half,
     xs_a, xr_a, xs_g, xr_g,
     as_a, ar_a, as_g, ar_g,
@@ -131,69 +132,87 @@
         return send_y, first, from_y, forward, last, sent
 
     def w_tools(w):
+        lo = SPLIT if w == WAVES - 1 else 0
+        rows = 128 - lo
         return ring_tools(
-            lambda b: wbuf.at[w, b], lambda b, way: wbuf.at[w, b, pl.ds(way * 64, 64)],
+            lambda b: wbuf.at[w, b, pl.ds(lo, rows)],
+            lambda b, way: wbuf.at[w, b, pl.ds(lo + way * (rows // 2), rows // 2)],
             lambda d: ws_y.at[w, d], lambda d, k, way: ws_z.at[w, d, k, way],
             lambda b: wr.at[w, b], lambda row: wr_half.at[w, row],
         )
 
-    w_send_y, w_first, w_from_y, w_forward, w_last, w_sent = zip(*[w_tools(w) for w in range(WAVES)])
-
-    def o_at(b):
-        return pl.ds(pl.multiple_of((b // 2) * 128, 128), 128), pl.ds(pl.multiple_of((b % 2) * 128, 128), 128)
-
-    def o_block(b):
-        return wo.at[(slice(None), *o_at(b))]
-
-    def o_half(b, way):
-        return wo.at[(way, *o_at(b))]
-
-    def o_spread(b, n):
+    def v_block(b):
+        return wbuf.at[WAVES - 1, b, pl.ds(0, SPLIT)]
+
+    def v_half(b, way):
+        return wbuf.at[WAVES - 1, b, pl.ds(way * (SPLIT // 2), SPLIT // 2)]
+
+    def v_spread(b, n):
         for d in range(1, NY):
-            send(o_block(b), o_block(b), os_y.at[n, d], orecv.at[b], tm_dev(wrap(y + d, NY), z))
-
-    def o_first():
-        @pl.when(swap_other)
-        def _():
-            await_bytes(o_block(t), orecv.at[t])
-
+            send(v_block(b), v_block(b), vs_y.at[n, d], vr.at[b], tm_dev(wrap(y + d, NY), z))
+
+    def v_first():
         for way, device in ((0, right), (1, left)):
-            send(o_block(t), o_block(t), os_z.at[0, way], orecv.at[t], device)
-        o_spread(t, 0)
-
-    def o_forward(k):
+            send(v_block(t), v_block(t), vs_z.at[0, way], vr.at[t], device)
+        v_spread(t, 0)
+
+    def v_forward(k):
         for way, (b, device) in enumerate(zip(ring_pair(0, k), (right, left))):
-            await_bytes(o_block(b), orecv.at[b])
+            await_bytes(v_block(b), vr.at[b])
             if k < HALF - 1:
-                send(o_block(b), o_block(b), os_z.at[k, way], orecv.at[b], device)
+                send(v_block(b), v_block(b), vs_z.at[k, way], vr.at[b], device)
             else:
-                rsem = orecv.at[b] if way == 0 else or_half.at[0]
-                send(o_half(b, way), o_half(b, way), os_z.at[k, way], rsem, device)
-            o_spread(b, 2 * k - 1 + way)
-
-    def o_last():
+                rsem = vr.at[b] if way == 0 else vr_half.at[0]
+                send(v_half(b, way), v_half(b, way), vs_z.at[k, way], rsem, device)
+            v_spread(b, 2 * k - 1 + way)
+
+    def v_last():
         b, _ = ring_pair(0, HALF)
-        await_bytes(o_half(b, 0), orecv.at[b])
-        await_bytes(o_half(b, 1), or_half.at[0])
-        o_spread(b, 7)
-
-    def o_all():
+        await_bytes(v_half(b, 0), vr.at[b])
+        await_bytes(v_half(b, 1), vr_half.at[0])
+        v_spread(b, 7)
+
+    def v_all():
         @pl.loop(1, NY)
         def _(d):
             for zz in range(NZ):
                 b = row_of(d) * NZ + zz
-                await_bytes(o_block(b), orecv.at[b])
-
-    def o_sent():
+                await_bytes(v_block(b), vr.at[b])
+
+    def v_sent():
         for way in range(2):
             for k in range(HALF - 1):
-                await_bytes(o_block(t), os_z.at[k, way])
-            await_bytes(o_half(t, 0), os_z.at[HALF - 1, way])
+                await_bytes(v_block(t), vs_z.at[k, way])
+            await_bytes(v_half(t, 0), vs_z.at[HALF - 1, way])
 
         @pl.loop(0, NZ)
         def _(n):
             for d in range(1, NY):
-                await_bytes(o_block(t), os_y.at[n, d])
+                await_bytes(v_block(t), vs_y.at[n, d])
+
+    w_send_y, w_first, w_from_y, w_forward, w_last, w_sent = zip(*[w_tools(w) for w in range(WAVES)])
+
+    def o_at(b):
+        return pl.ds(pl.multiple_of((b // 2) * 128, 128), 128), pl.ds(pl.multiple_of((b % 2) * 128, 128), 128)
+
+    def o_block(b):
+        return wo.at[(slice(None), *o_at(b))]
+
+    o_send_y, o_first, o_from_y, o_forward, o_last, o_sent = ring_tools(
+        o_block, lambda b, way: wo.at[(way, *o_at(b))],
+        lambda d: os_y.at[d], lambda d, k, way: os_z.at[d, k, way],
+        lambda b: orecv.at[b], lambda row: or_half.at[row],
+    )
+
+    def o_swapped():
+        @pl.when(swap_other)
+        def _():
+            await_bytes(o_block(t), orecv.at[t])
+
+    def o_all():
+        @pl.loop(0, NY)
+        def _(d):
+            o_last(d)
 
     def multiply(w):
         @pl.loop(0, NY)
@@ -202,14 +221,12 @@
             row = row_of(d)
             depth = NZ * 128
 
-            @pl.loop(0, 2)
-            def _(r):
-                total = jnp.dot(
-                    xall[pl.ds(pl.multiple_of(r * 256, 256), 256), pl.ds(pl.multiple_of(row * depth, depth), depth)],
-                    wbuf[w, pl.ds(row * NZ, NZ)].reshape(depth, 3 * CW),
-                    preferred_element_type=jnp.float32,
-                )
-                acc[w, pl.ds(r * 8, 8)] = acc[w, pl.ds(r * 8, 8)] + total.reshape(8, 32, 3 * CW)
+            total = jnp.dot(
+                xall[:, pl.ds(pl.multiple_of(row * depth, depth), depth)],
+                wbuf[w, pl.ds(row * NZ, NZ)].reshape(depth, 3 * CW),
+                preferred_element_type=jnp.float32,
+            )
+            acc[w] = acc[w] + total.reshape(16, 32, 3 * CW)
 
     def near(first, block, index, ssem, rsem):
         devices = [tensor_dev(x, h, 1 - c)]
@@ -353,38 +370,46 @@
         send(nbuf.at[zz], x_rows(j, z * 64, 64), xs_a.at[d], xr_a.at[z], tm_dev(y, zz))
 
     w_from_y[0]()
+    v_first()
     x_pieces()
     gather_own(x_block, x_ss, x_rs)
     w_forward[0](1)
+    gather_partner(x_block, x_ss, x_rs)
     w_send_y[1]()
+    v_forward(1)
     w_forward[0](2)
-    gather_partner(x_block, x_ss, x_rs)
-    o_first()
+    v_forward(2)
     w_forward[0](3)
     w_from_y[1]()
-    o_forward(1)
+    v_forward(3)
     gather_x(x_block, x_ss, x_rs)
-    w_forward[1](1)
     gather_sibling(x_block, x_rs)
-    o_forward(2)
     multiply(0)
     attention(0)
+    w_forward[1](1)
+    v_last()
+    o_swapped()
+    o_send_y()
     w_forward[1](2)
-    o_forward(3)
     a_pieces(0)
     gather_own(*a_tools(0))
     w_forward[1](3)
-    o_last()
+    o_first(0)
+    o_from_y()
+    v_all()
     gather_partner(*a_tools(0))
     multiply(1)
     attention(1)
-    gather_x(*a_tools(0))
+    o_forward(1)
     a_pieces(1)
     gather_own(*a_tools(1))
+    gather_x(*a_tools(0))
+    o_forward(2)
+    gather_partner(*a_tools(1))
     gather_sibling(a_tools(0)[0], a_tools(0)[2])
+    o_forward(3)
     o_all()
     project(0)
-    gather_partner(*a_tools(1))
     gather_x(*a_tools(1))
     gather_sibling(a_tools(1)[0], a_tools(1)[2])
     project(1)
@@ -403,6 +428,7 @@
         def _(n):
             await_bytes(a_rows(w, 0, 0, 512), as_g.at[w, n])
 
+    v_sent()
     o_sent()
 
     @pl.when(swap_other)
@@ -439,7 +465,8 @@
             pltpu.VMEM((WAVES, count, 16 * CW), bf16),
             pltpu.VMEM((count, 256), f32),
             dma, dma((WAVES, NY, HALF, 2)), dma((WAVES, NY)), dma((WAVES, NY * NZ)), dma((WAVES, NY)),
-            dma((HALF, 2)), dma((NZ, NY)), dma((1,)), dma((NY * NZ,)), dma((1,)),
+            dma((HALF, 2)), dma((NZ, NY)), dma((NY * NZ,)), dma((1,)),
+            dma((NY, HALF, 2)), dma((NY,)), dma((1,)), dma((NY * NZ,)), dma((NY,)),
             dma((NZ,)), dma((NZ,)), dma((15,)), dma((16,)),
             dma((WAVES, NZ)), dma((WAVES, NZ)), dma((WAVES, 15)), dma((WAVES, 16)),
         ],

time: 131 us -> 124 us (0.947)
  Pallas kernels: 128 us -> 121 us
    pallas_call x1, Pallas kernels: 128 us -> 121 us  [body(): pl.pallas_call(kernel, out_shape=jax.ShapeDtypeStruct((frames_dev, patche...]
where the time goes in v4:
time: 124 us; the launch traced here: 123 us
  Pallas kernels  121 us (98%)
  local copies, waits for them, and re-layouts  1.67 us (1%)
    pallas_call x1, Pallas kernels, body(): pl.pallas_call(kernel, out_shape=jax.ShapeDtypeStruct((frames_dev, patche...  121 us

profile of v4, /device:TPU:1, one launch (start us, length us, event | category | flops | bytes accessed | tf_op | source)
XLA Modules:
  0.0 122.7 jit_solution(12663591945288614352)
XLA Ops:
  0.0 121.0 %shard_map.64 = bf16[2,256,256]{2,1,0:T(8,128)(2,1)} custom-call(bf16[512,4096]{1,0:T(8,128)(2,1)} %bitcast.3, f32[1,4096]{1,0:T(1,128)} %bitcast.5, f32[2,128]{1,0:T(2,128)} %qg_ref.1, f32[2,128]{1,0:T(2,128)} %kg_ref.1, bf16[3,128,256]{2,1,0:T(8,128)(2,1)} %wq_ref.1, bf16[2,128,128]{2,1,0:T(8,128)(2,1)} %bitcast.4), custom_call_target="tpu_custom_call" | custom-call | flops 4294967296 | bytes 16777216 | tf_op jit(solution)/shard_map/pallas_call | solution.py:452
  121.0 1.7 %copy.8 = bf16[2,256,256]{2,1,0:T(8,128)(2,1)} copy(bf16[2,256,256]{2,1,0:T(8,128)(2,1)} %shard_map.64) | data formatting | bytes 524288

commit v5 on v4

--- a/solution.py
+++ b/solution.py
@@ -13,7 +13,7 @@
 HPW = 2 // WAVES
 CW = 128 * HPW
 HALF = NZ // 2
-SPLIT = 32
+SPLIT = 64
 
 
 def wrap(value, size):
@@ -147,9 +147,25 @@
     def v_half(b, way):
         return wbuf.at[WAVES - 1, b, pl.ds(way * (SPLIT // 2), SPLIT // 2)]
 
+    far_row = jnp.where(y == 1, NY - 1, 0)
+    relays = jnp.logical_or(y == 1, y == 2)
+
     def v_spread(b, n):
         for d in range(1, NY):
-            send(v_block(b), v_block(b), vs_y.at[n, d], vr.at[b], tm_dev(wrap(y + d, NY), z))
+            to = row_of(d)
+
+            @pl.when(jnp.logical_or(relays, to + y != NY - 1))
+            def _():
+                send(v_block(b), v_block(b), vs_y.at[n, d], vr.at[b], tm_dev(to, z))
+
+    def v_far(n):
+        away = (n + 1) // 2
+        b = far_row * NZ + wrap(z - away if n % 2 else z + away, NZ)
+
+        @pl.when(relays)
+        def _():
+            await_bytes(v_block(b), vr.at[b])
+            send(v_block(b), v_block(b), vs_y.at[n, 0], vr.at[b], tm_dev(NY - 1 - far_row, z))
 
     def v_first():
         for way, device in ((0, right), (1, left)):
@@ -175,9 +191,13 @@
     def v_all():
         @pl.loop(1, NY)
         def _(d):
-            for zz in range(NZ):
-                b = row_of(d) * NZ + zz
-                await_bytes(v_block(b), vr.at[b])
+            row = row_of(d)
+
+            @pl.when(jnp.logical_not(jnp.logical_and(relays, row == far_row)))
+            def _():
+                for zz in range(NZ):
+                    b = row * NZ + zz
+                    await_bytes(v_block(b), vr.at[b])
 
     def v_sent():
         for way in range(2):
@@ -188,7 +208,13 @@
         @pl.loop(0, NZ)
         def _(n):
             for d in range(1, NY):
-                await_bytes(v_block(t), vs_y.at[n, d])
+                @pl.when(jnp.logical_or(relays, row_of(d) + y != NY - 1))
+                def _():
+                    await_bytes(v_block(t), vs_y.at[n, d])
+
+            @pl.when(relays)
+            def _():
+                await_bytes(v_block(t), vs_y.at[n, 0])
 
     w_send_y, w_first, w_from_y, w_forward, w_last, w_sent = zip(*[w_tools(w) for w in range(WAVES)])
 
@@ -224,6 +250,22 @@
             total = jnp.dot(
                 xall[:, pl.ds(pl.multiple_of(row * depth, depth), depth)],
                 wbuf[w, pl.ds(row * NZ, NZ)].reshape(depth, 3 * CW),
+                preferred_element_type=jnp.float32,
+            )
+            acc[w] = acc[w] + total.reshape(16, 32, 3 * CW)
+
+    def multiply_half(w, late):
+        @pl.loop(0, NY)
+        def _(d):
+            if late:
+                w_last[w](d)
+            near = z // HALF
+            start = row_of(d) * NZ + HALF * (1 - near if late else near)
+            depth = HALF * 128
+
+            total = jnp.dot(
+                xall[:, pl.ds(pl.multiple_of(start * 128, depth), depth)],
+                wbuf[w, pl.ds(start, HALF)].reshape(depth, 3 * CW),
                 preferred_element_type=jnp.float32,
             )
             acc[w] = acc[w] + total.reshape(16, 32, 3 * CW)
@@ -377,37 +419,46 @@
     gather_partner(x_block, x_ss, x_rs)
     w_send_y[1]()
     v_forward(1)
+    v_far(0)
     w_forward[0](2)
     v_forward(2)
+    o_swapped()
+    o_send_y()
     w_forward[0](3)
     w_from_y[1]()
     v_forward(3)
+    v_far(1)
+    v_far(2)
     gather_x(x_block, x_ss, x_rs)
     gather_sibling(x_block, x_rs)
     multiply(0)
     attention(0)
     w_forward[1](1)
+    v_far(3)
+    v_far(4)
     v_last()
-    o_swapped()
-    o_send_y()
-    w_forward[1](2)
     a_pieces(0)
     gather_own(*a_tools(0))
+    w_forward[1](2)
+    v_far(5)
+    v_far(6)
+    v_far(7)
     w_forward[1](3)
     o_first(0)
     o_from_y()
+    gather_partner(*a_tools(0))
     v_all()
-    gather_partner(*a_tools(0))
-    multiply(1)
+    multiply_half(1, False)
+    multiply_half(1, True)
     attention(1)
     o_forward(1)
     a_pieces(1)
     gather_own(*a_tools(1))
+    o_forward(2)
     gather_x(*a_tools(0))
-    o_forward(2)
     gather_partner(*a_tools(1))
+    o_forward(3)
     gather_sibling(a_tools(0)[0], a_tools(0)[2])
-    o_forward(3)
     o_all()
     project(0)
     gather_x(*a_tools(1))

time: 124 us -> 121 us (0.976); the launches traced: 123 us -> 121 us
  Pallas kernels: 121 us -> 119 us
    pallas_call x1, Pallas kernels: 121 us -> 119 us  [body(): pl.pallas_call(kernel, out_shape=jax.ShapeDtypeStruct((frames_dev, patche...]
where the time goes in v5:
time: 121 us
  Pallas kernels  119 us (98%)
  local copies, waits for them, and re-layouts  1.67 us (1%)
    pallas_call x1, Pallas kernels, body(): pl.pallas_call(kernel, out_shape=jax.ShapeDtypeStruct((frames_dev, patche...  119 us

profile of v5, /device:TPU:1, one launch (start us, length us, event | category | flops | bytes accessed | tf_op | source)
XLA Modules:
  0.0 121.0 jit_solution(3525072021424874003)
XLA Ops:
  0.0 119.3 %shard_map.64 = bf16[2,256,256]{2,1,0:T(8,128)(2,1)} custom-call(bf16[512,4096]{1,0:T(8,128)(2,1)} %bitcast.3, f32[1,4096]{1,0:T(1,128)} %bitcast.5, f32[2,128]{1,0:T(2,128)} %qg_ref.1, f32[2,128]{1,0:T(2,128)} %kg_ref.1, bf16[3,128,256]{2,1,0:T(8,128)(2,1)} %wq_ref.1, bf16[2,128,128]{2,1,0:T(8,128)(2,1)} %bitcast.4), custom_call_target="tpu_custom_call" | custom-call | flops 4294967296 | bytes 16777216 | tf_op jit(solution)/shard_map/pallas_call | solution.py:503
  119.3 1.7 %copy.8 = bf16[2,256,256]{2,1,0:T(8,128)(2,1)} copy(bf16[2,256,256]{2,1,0:T(8,128)(2,1)} %shard_map.64) | data formatting | bytes 524288
